TPU v7x, 256 devices: a whole 4x4x8 slice. The times are simulated.
256 devices in a mesh: row: 8 (over x, core), col: 32 (over y, z).
Axes of the slice: x: 4, y: 4, z: 8, core: 2. Of those that a mesh axis runs over, the one named last changes fastest.
Arguments:
- features: bfloat16 [65536, 256], P(('row', 'col')), may hold values from -6 to 6
- neighbours: int32 [10, 65536], P(None, ('row', 'col')), may hold values from 0 to 511, as said below
- halo_ids: int32 [256, 1, 256], P(('row', 'col')), may hold values from 0 to 255
- w_self: bfloat16 [256, 256], replicated, may hold values from -0.375 to 0.375
- w_neigh: bfloat16 [256, 256], replicated, may hold values from -0.75 to 0.75
- b_sage: float32 [256], replicated, may hold values from -3 to 3
- w_first: bfloat16 [512, 256], replicated, may hold values from -0.25 to 0.25
- b_first: float32 [256], replicated, may hold values from -3 to 3
- w_second: bfloat16 [256], replicated, may hold values from -1.5 to 1.5
- b_second: float32 [1], replicated, may hold values from -3 to 3
- src_owner: int32 [8, 32, 8192, 1], P('row', 'col'), may hold values from 0 to 31; in each aligned block of 8192 rows (0 to 8191, 8192 to 16383, ..., all dimensions but the last counted through in order) at most 320 rows name the same one
- src_local: int32 [8, 32, 8192], P('row', 'col'), may hold values from 0 to 255
- dst_index: int32 [8, 32, 8192], P('row', 'col'), may hold values from 0 to 2047
- labels: int32 [8, 32, 8192], P('row', 'col'), may hold values 0 or 1
Outputs:
- embeds: bfloat16 [65536, 256], P(('row', 'col'))
- logits: float32 [8, 32, 8192], P('row', 'col')
- node_grad: float32 [65536, 256], P(('row', 'col'))
- grad_self: float32 [256, 256], replicated
- grad_neigh: float32 [256, 256], replicated
- grad_bsage: float32 [256], replicated
- grad_first: float32 [32, 512, 256], P('col')
- grad_bfirst: float32 [32, 256], P('col')
- grad_second: float32 [32, 256], P('col')
Inputs may be any that keep to these rules, and one draw needn't show every extreme that they name: `neighbours`: in each partition every one of the 256 received rows (values 256 and up) is named by exactly one entry; the other entries name the partition's own rows. `src_owner`: among the 8192 edges of one tile at most 320 name the same source partition, and that many are reached.
All inputs are finite; a program needn't handle non-finite values. No bound on the sum of `labels` on one device may be relied on, other than what follows from the above.
Results may differ from a plain program's by a relative error of at most 0.0052.
Values may be sent and summed in bfloat16 or wider, within the bound.
No kernel may reach another device: no remote copies, remote signals or barrier semaphores. Data moves between devices by JAX's collectives and lax.ppermute only.
A program may use at most 128 MiB of HBM per device.

v0:
```python
import jax
import jax.numpy as jnp
from jax import lax
from jax.sharding import PartitionSpec as P


def per_device(
    features,
    neighbours,
    halo_ids,
    w_self,
    w_neigh,
    b_sage,
    w_first,
    b_first,
    w_second,
    b_second,
    src_owner,
    src_local,
    dst_index,
    labels,
):
    node_dev, feat_width = features.shape
    fanout = neighbours.shape[0]
    row_count = lax.axis_size("row")
    col_count = lax.axis_size("col")
    outgoing = features[halo_ids[0]]
    halo_count = outgoing.shape[0]
    outgoing = outgoing.reshape(halo_count, row_count, col_count, feat_width)
    received = lax.all_to_all(
        lax.all_to_all(outgoing, "row", split_axis=1, concat_axis=1, tiled=True),
        "col",
        split_axis=2,
        concat_axis=2,
        tiled=True,
    )
    extended = jnp.concatenate([features, received.reshape(-1, feat_width)], axis=0)
    gathered = extended[neighbours].astype(jnp.float32)
    aggregate = (jnp.sum(gathered, axis=0) / fanout).astype(jnp.bfloat16)
    embed_f = jnp.dot(features, w_self, preferred_element_type=jnp.float32)
    embed_f = embed_f + jnp.dot(aggregate, w_neigh, preferred_element_type=jnp.float32) + b_sage
    embeds = embed_f.astype(jnp.bfloat16)
    owners = src_owner[0, 0, :, 0]
    local_rows = src_local[0, 0]
    dest_rows = dst_index[0, 0]
    targets = labels[0, 0].astype(jnp.float32)
    edge_count = owners.shape[0]
    src_block = lax.all_gather(embeds, "col", axis=0, tiled=True)
    block_rows = owners * node_dev + local_rows
    src_embed = src_block[block_rows]
    dst_block = lax.all_gather(embeds, "row", axis=0, tiled=True)
    dst_embed = dst_block[dest_rows]
    w_src = w_first[:feat_width]
    w_dst = w_first[feat_width:]
    preact = jnp.dot(src_embed, w_src, preferred_element_type=jnp.float32)
    preact = preact + jnp.dot(dst_embed, w_dst, preferred_element_type=jnp.float32) + b_first
    gate_sig = jax.nn.sigmoid(preact)
    hidden = preact * gate_sig
    hidden_b = hidden.astype(jnp.bfloat16)
    logits = jnp.dot(hidden_b, w_second, preferred_element_type=jnp.float32) + b_second[0]
    dlogit = jax.nn.sigmoid(logits) - targets
    second_f = w_second.astype(jnp.float32)
    dpreact = dlogit[:, None] * second_f[None, :] * gate_sig * (1.0 + preact * (1.0 - gate_sig))
    dpreact_b = dpreact.astype(jnp.bfloat16)
    part_second = jnp.sum(hidden * dlogit[:, None], axis=0)
    part_bfirst = jnp.sum(dpreact, axis=0)
    grad_src = jnp.dot(src_embed.T, dpreact_b, preferred_element_type=jnp.float32)
    grad_dst = jnp.dot(dst_embed.T, dpreact_b, preferred_element_type=jnp.float32)
    part_first = jnp.concatenate([grad_src, grad_dst], axis=0)
    decoder_sums = lax.psum((part_first, part_bfirst, part_second), "row")
    src_rows_g = jnp.dot(dpreact_b, w_src.T, preferred_element_type=jnp.float32).astype(
        jnp.bfloat16
    )
    dst_rows_g = jnp.dot(dpreact_b, w_dst.T, preferred_element_type=jnp.float32).astype(
        jnp.bfloat16
    )
    src_acc = (
        jnp.zeros((src_block.shape[0], feat_width), jnp.float32)
        .at[block_rows]
        .add(src_rows_g.astype(jnp.float32))
    )
    src_grad = lax.psum_scatter(src_acc, "col", scatter_dimension=0, tiled=True)
    dest_acc = (
        jnp.zeros((dst_block.shape[0], feat_width), jnp.float32)
        .at[dest_rows]
        .add(dst_rows_g.astype(jnp.float32))
    )
    dest_grad = lax.psum_scatter(dest_acc, "row", scatter_dimension=0, tiled=True)
    node_grad = src_grad + dest_grad
    node_grad_b = node_grad.astype(jnp.bfloat16)
    part_self = jnp.dot(features.T, node_grad_b, preferred_element_type=jnp.float32)
    part_neigh = jnp.dot(aggregate.T, node_grad_b, preferred_element_type=jnp.float32)
    part_bsage = jnp.sum(node_grad, axis=0)
    encoder_sums = lax.psum((part_self, part_neigh, part_bsage), ("row", "col"))
    return (
        embeds,
        logits.reshape(1, 1, edge_count),
        node_grad,
        encoder_sums[0],
        encoder_sums[1],
        encoder_sums[2],
        decoder_sums[0][None],
        decoder_sums[1][None],
        decoder_sums[2][None],
    )


def solution(mesh):
    placed = (
        P(("row", "col"), None),
        P(None, ("row", "col")),
        P(("row", "col"), None, None),
        P(),
        P(),
        P(),
        P(),
        P(),
        P(),
        P(),
        P("row", "col", None, None),
        P("row", "col", None),
        P("row", "col", None),
        P("row", "col", None),
    )
    return jax.shard_map(
        per_device,
        mesh=mesh,
        in_specs=placed,
        out_specs=(
            P(("row", "col"), None),
            P("row", "col", None),
            P(("row", "col"), None),
            P(),
            P(),
            P(),
            P("col", None, None),
            P("col", None),
            P("col", None),
        ),
        check_vma=False,
    )
```

profile of v0, /device:TPU:8, one launch (start us, length us, event | category | flops | bytes accessed | tf_op | source)
XLA Modules:
  0.0 875.0 jit_solution(14454785513505962907)
XLA Ops:
  7.2 0.0 copy-start
  7.2 0.0 copy-start.13
  7.2 0.0 copy-start.7
  7.2 0.7 compare_select_fusion.3
  8.0 2.5 gather_fusion
  10.5 0.0 copy-start.11
  10.5 4.4 all-to-all-start
  15.0 0.7 compare_select_fusion.2
  15.7 5.4 all-to-all-done
  21.1 0.7 copy.26
  21.8 11.7 %all-to-all-start.1 = ((bf16[1,8,32,256]{3,1,0,2:T(8,128)(2,1)}), bf16[1,8,32,256]{3,1,0,2:T(8,128)(2,1)S(1)}, u32[]{:S(2)}, u32[]{:S(2)}) async-start(bf16[1,8,32,256]{3,1,0,2:T(8,128)(2,1)} %copy.26), calls=%async_computation.1 | async-start | bytes 262144 | tf_op jit(solution)/shard_map/all_to_all | solution.py:30
  33.6 0.0 all-gather.5.cloned.1.call-start
  33.6 1.1 fusion.26
  34.7 7.9 all-to-all-done.1
  42.7 0.9 pad_maximum_fusion
  43.6 7.6 gather_fusion.1
  51.2 0.2 convert_reduce_fusion
  51.4 0.9 fusion.10
  52.2 0.0 all-gather.5.cloned.1.call-update
  52.3 0.0 all-gather.3.cloned.1.call-start
  52.3 0.7 all-gather.3.cloned.1.call-update
  53.0 0.2 reduce-scatter.5.cloned.1.call-start
  53.2 0.0 copy-done.14
  53.9 0.0 copy-done.10
  54.0 0.1 compare_select_fusion.1
  54.1 18.4 %all-gather.5.cloned.1.call-done = bf16[2048,256]{1,0:T(8,128)(2,1)} async-done(((bf16[256,256]{1,0:T(8,128)(2,1)}), bf16[2048,256]{1,0:T(8,128)(2,1)}) %all-gather.5.cloned.1.call-update) | async-done | bytes 1048592 | tf_op jit(solution)/shard_map/all_gather | solution.py:51
  72.6 32.2 %gather_fusion.3 = bf16[8192,256]{1,0:T(8,128)(2,1)} fusion(bf16[2048,256]{1,0:T(8,128)(2,1)} %all-gather.5.cloned.1.call-done, s32[8192]{0:T(1024)S(1)} %broadcast_clamp_fusion), kind=kCustom, calls=%fused_computation.3 | custom fusion | bytes 8421376 | tf_op jit(solution)/shard_map/gather | solution.py:52
  104.8 51.4 %all-gather.3.cloned.1.call-done = bf16[8192,256]{1,0:T(8,128)(2,1)} async-done(((bf16[256,256]{1,0:T(8,128)(2,1)}), bf16[8192,256]{1,0:T(8,128)(2,1)}) %all-gather.3.cloned.1.call-update) | async-done | bytes 4194320 | tf_op jit(solution)/shard_map/all_gather | solution.py:48
  156.2 33.6 %gather_fusion.2 = bf16[8192,256]{1,0:T(8,128)(2,1)} fusion(bf16[8192,256]{1,0:T(8,128)(2,1)} %all-gather.3.cloned.1.call-done, s32[8192]{0:T(1024)S(1)} %broadcast_clamp_fusion.1), kind=kCustom, calls=%fused_computation.2 | custom fusion | bytes 8421376 | tf_op jit(solution)/shard_map/gather | solution.py:50
  189.8 0.0 copy-done.6
  189.8 3.6 fusion.16
  193.4 1.3 fusion
  194.7 2.4 fusion.6
  197.1 0.6 divide_subtract_fusion
  197.8 5.9 fusion.24
  203.6 2.0 copy-done.2
  205.6 4.5 fusion.1
  210.1 46.0 %scatter_custom_fusion.1 = f32[2048,256]{1,0:T(8,128)} fusion(s32[8192]{0:T(1024)S(1)} %bitcast.48, f32[8192,256]{1,0:T(8,128)} %fusion.1, f32[]{:T(128)} %constant.11.clone.1), kind=kCustom, calls=%fused_computation.25 | custom fusion | flops 2097152 | bytes 2097664 | tf_op jit(solution)/shard_map/scatter-add | solution.py:86
  256.1 0.0 reduce-scatter.5.cloned.1.call-update
  256.2 0.3 reduce-scatter.3.cloned.1.call-start
  256.4 6.7 fusion.2
  263.1 48.3 %scatter_custom_fusion = f32[8192,256]{1,0:T(8,128)} fusion(s32[8192]{0:T(1024)S(1)} %bitcast.46, f32[8192,256]{1,0:T(8,128)} %fusion.2, f32[]{:T(128)} %constant.11.clone.1), kind=kCustom, calls=%fused_computation.16 | custom fusion | flops 2097152 | bytes 8389120 | tf_op jit(solution)/shard_map/scatter-add | solution.py:80
  311.5 0.0 reduce-scatter.3.cloned.1.call-update
  311.5 0.0 copy-start.4
  311.5 0.0 all-reduce.7.cloned.1.call-start
  311.5 4.8 fusion.27
  316.3 0.0 reduce-scatter.5.cloned.1.call-done
  316.3 221.9 %reduce-scatter.3.cloned.1.call-done = f32[256,256]{1,0:T(8,128)} async-done(((f32[8192,256]{1,0:T(8,128)}), f32[256,256]{1,0:T(8,128)}) %reduce-scatter.3.cloned.1.call-update) | async-done | bytes 262160 | tf_op jit(solution)/shard_map/reduce_scatter | solution.py:82
  538.3 1.1 fusion.25
  539.4 0.9 fusion.18
  540.3 0.9 convolution_bitcast_fusion
  541.3 0.0 all-reduce.7.cloned.1.call-update
  541.3 0.0 copy-start.1
  541.3 0.0 all-reduce.5.cloned.1.call-start
  541.3 4.8 fusion.28
  546.1 0.8 maximum_bitcast_fusion
  547.0 0.0 all-reduce.5.cloned.1.call-update
  547.0 13.0 %all-reduce.1 = (f32[1,256]{1,0:T(1,128)}, f32[1,256]{1,0:T(1,128)}) all-reduce(f32[1,256]{1,0:T(1,128)S(1)} %bitcast.52, f32[1,256]{1,0:T(1,128)S(1)} %bitcast.53), channel_id=1, replica_groups=mesh['row'=8,'col'=32] {'row'}, use_global_device_ids=true, to_apply=%region_11.0 | all-reduce | flops 512 | bytes 4096 | tf_op jit(solution)/shard_map/psum | solution.py:70
  560.0 74.7 %psum.44 = f32[256]{0:T(256)} all-reduce(f32[256]{0:T(256)S(1)} %get-tuple-element.42), channel_id=1, replica_groups=mesh['row'=8,'col'=32] {'row','col'}, use_global_device_ids=true, to_apply=%region_8.0 | all-reduce | flops 256 | bytes 2048 | tf_op jit(solution)/shard_map/psum | solution.py:94
  634.6 162.6 %all-reduce.7.cloned.1.call-done = (f32[256,256]{0,1:T(8,128)}, f32[256,256]{1,0:T(8,128)}) async-done(((f32[256,256]{0,1:T(8,128)}, f32[256,256]{1,0:T(8,128)}), (f32[256,256]{0,1:T(8,128)}, f32[256,256]{1,0:T(8,128)})) %all-reduce.7.cloned.1.call-update) | async-done | bytes 524304 | tf_op jit(solution)/shard_map/psum | solution.py:94
  797.2 1.8 copy.28
  799.0 65.6 %all-reduce.5.cloned.1.call-done = f32[1,512,256]{2,1,0:T(8,128)} async-done(((f32[1,512,256]{2,1,0:T(8,128)}), f32[1,512,256]{2,1,0:T(8,128)}) %all-reduce.5.cloned.1.call-update) | async-done | bytes 524304 | tf_op jit(solution)/shard_map/psum | solution.py:70
  864.6 1.7 copy.33
  866.2 1.9 copy.34
  (30 shorter events, 0.2 us)
Async XLA Ops:
  7.2 26.4 %copy-start = (bf16[256,256]{1,0:T(8,128)(2,1)S(1)}, bf16[256,256]{1,0:T(8,128)(2,1)}, u32[]{:S(2)}) copy-start(bf16[256,256]{1,0:T(8,128)(2,1)} %param.17) | copy-start | bytes 393220
  7.2 44.2 %copy-start.13 = (f32[256]{0:T(256)S(1)}, f32[256]{0:T(256)}, u32[]{:S(2)}) copy-start(f32[256]{0:T(256)} %param.19) | copy-start | bytes 3076
  7.2 44.2 %copy-start.7 = (bf16[256,256]{1,0:T(8,128)(2,1)S(1)}, bf16[256,256]{1,0:T(8,128)(2,1)}, u32[]{:S(2)}) copy-start(bf16[256,256]{1,0:T(8,128)(2,1)} %param.18) | copy-start | bytes 393220
  10.5 42.7 %copy-start.14 = (bf16[256]{0:T(256)(128)(2,1)S(1)}, bf16[256]{0:T(256)(128)(2,1)}, u32[]{:S(2)}) copy-start(bf16[256]{0:T(256)(128)(2,1)} %param.22) | copy-start | bytes 1540
  10.5 43.4 %copy-start.10 = (s32[1,1,8192]{2,1,0:T(1,128)S(1)}, s32[1,1,8192]{2,1,0:T(1,128)}, u32[]{:S(2)}) copy-start(s32[1,1,8192]{2,1,0:T(1,128)} %param.27) | copy-start | bytes 98308
  10.5 43.4 %copy-start.8 = (s32[1,1,8192]{2,1,0:T(1,128)S(1)}, s32[1,1,8192]{2,1,0:T(1,128)}, u32[]{:S(2)}) copy-start(s32[1,1,8192]{2,1,0:T(1,128)} %param.25) | copy-start | bytes 98308
  10.5 43.5 %copy-start.9 = (s32[1,1,8192,1]{2,3,1,0:T(1,128)S(1)}, s32[1,1,8192,1]{2,3,1,0:T(1,128)}, u32[]{:S(2)}) copy-start(s32[1,1,8192,1]{2,3,1,0:T(1,128)} %param.24) | copy-start | bytes 98308
  10.5 43.5 %copy-start.11 = (s32[1,1,8192]{2,1,0:T(1,128)S(1)}, s32[1,1,8192]{2,1,0:T(1,128)}, u32[]{:S(2)}) copy-start(s32[1,1,8192]{2,1,0:T(1,128)} %param.26) | copy-start | bytes 98308
  10.5 10.6 %all-to-all-start = ((bf16[1,8,32,256]{3,2,0,1:T(8,128)(2,1)}), bf16[1,8,32,256]{3,2,0,1:T(8,128)(2,1)S(1)}, u32[]{:S(2)}, u32[]{:S(2)}) async-start(bf16[1,8,32,256]{3,2,0,1:T(8,128)(2,1)} %bitcast.3), calls=%async_computation | async-start | bytes 262144 | tf_op jit(solution)/shard_map/all_to_all | solution.py:31
  21.8 20.8 %all-to-all-start.1 = ((bf16[1,8,32,256]{3,1,0,2:T(8,128)(2,1)}), bf16[1,8,32,256]{3,1,0,2:T(8,128)(2,1)S(1)}, u32[]{:S(2)}, u32[]{:S(2)}) async-start(bf16[1,8,32,256]{3,1,0,2:T(8,128)(2,1)} %copy.26), calls=%async_computation.1 | async-start | bytes 262144 | tf_op jit(solution)/shard_map/all_to_all | solution.py:30
  33.6 39.0 %all-gather.5.cloned.1.call-start = ((), (), s32[]{:S(2)}) async-start(), calls=%async_computation.5 | async-start | bytes 1179648 | tf_op jit(solution)/shard_map/all_gather | solution.py:51
  52.3 103.9 %all-gather.3.cloned.1.call-start = ((), (), s32[]{:S(2)}) async-start(), calls=%async_computation.4 | async-start | bytes 4325376 | tf_op jit(solution)/shard_map/all_gather | solution.py:48
  53.0 263.3 %reduce-scatter.5.cloned.1.call-start = ((), (), s32[]{:S(2)}) async-start(), calls=%async_computation.7 | async-start | bytes 2359296 | tf_op jit(solution)/shard_map/reduce_scatter | solution.py:88
  104.8 85.0 %copy-start.6 = (bf16[512,256]{1,0:T(8,128)(2,1)S(1)}, bf16[512,256]{1,0:T(8,128)(2,1)}, u32[]{:S(2)}) copy-start(bf16[512,256]{1,0:T(8,128)(2,1)} %param.20) | copy-start | bytes 786436
  189.8 3.6 copy-start.3
  189.8 3.6 copy-start.12
  203.6 2.0 copy-start.2
  256.2 282.1 %reduce-scatter.3.cloned.1.call-start = ((), (), s32[]{:S(2)}) async-start(), calls=%async_computation.6 | async-start | bytes 8650752 | tf_op jit(solution)/shard_map/reduce_scatter | solution.py:82
  311.5 228.8 %copy-start.4 = (bf16[256,256]{1,0:T(8,128)(2,1)S(1)}, bf16[256,256]{1,0:T(8,128)(2,1)}, u32[]{:S(2)}) copy-start(bf16[256,256]{1,0:T(8,128)(2,1)} %param.14) | copy-start | bytes 393220
  311.5 485.7 %all-reduce.7.cloned.1.call-start = ((), (), s32[]{:S(2)}) async-start(), calls=%async_computation.9 | async-start | bytes 1048576 | tf_op jit(solution)/shard_map/psum | solution.py:94
  539.4 6.7 copy-start.5
  541.3 326.8 %copy-start.1 = (bf16[256,256]{1,0:T(8,128)(2,1)S(1)}, bf16[256,256]{1,0:T(8,128)(2,1)}, u32[]{:S(2)}) copy-start(bf16[256,256]{1,0:T(8,128)(2,1)} %param.17) | copy-start | bytes 393220
  541.3 323.3 %all-reduce.5.cloned.1.call-start = ((), (), s32[]{:S(2)}) async-start(), calls=%async_computation.8 | async-start | bytes 1048576 | tf_op jit(solution)/shard_map/psum | solution.py:70
Sparse Core Ops, SparseCore 0:
  52.4 20.1 all-gather.4
  75.7 80.4 all-gather.2
  256.3 34.6 reduce-scatter.4
  311.6 226.6 reduce-scatter.2
  545.3 251.9 all-reduce.6
  800.1 64.4 all-reduce.4
where the time goes:
time: 876 us; the launch traced here: 875 us
  waiting for transfers between devices  534 us (61%)
  other arithmetic  105 us (12%)
  blocking collectives  87.7 us (10%)
  local copies, waits for them, and re-layouts  84.1 us (10%)
  matrix products  31.8 us (4%)
  starting transfers between devices  16.8 us (2%)
  between operations  15.1 us (2%)
    reduce_scatter x1, waiting for transfers between devices, per_device(): src_grad = lax.psum_scatter(src_acc, 'col', scatter_dimension=0, tiled=True)  222 us
    psum x1, waiting for transfers between devices, per_device(): encoder_sums = lax.psum((part_self, part_neigh, part_bsage), ('row', 'col'))  163 us
    psum x1, blocking collectives, per_device(): encoder_sums = lax.psum((part_self, part_neigh, part_bsage), ('row', 'col'))  74.7 us
    psum x1, waiting for transfers between devices, per_device(): decoder_sums = lax.psum((part_first, part_bfirst, part_second), 'row')  65.6 us
    all_gather x1, waiting for transfers between devices, per_device(): src_block = lax.all_gather(embeds, 'col', axis=0, tiled=True)  51.4 us
    scatter-add x1, other arithmetic, per_device(): src_acc = jnp.zeros((src_block.shape[0], feat_width), jnp.float32).at[blo...  48.3 us
    scatter-add x1, other arithmetic, per_device(): dest_acc = jnp.zeros((dst_block.shape[0], feat_width), jnp.float32).at[de...  46 us
    gather x1, local copies, waits for them, and re-layouts, per_device(): src_embed = src_block[block_rows]  33.6 us
  transfers between devices with their start and end apart: 8, of which 7 were waited for; matrix products, arithmetic and copies ran while one was open for 12% of the time, Pallas kernels for 0%

commit v1 on v0

--- a/solution.py
+++ b/solution.py
@@ -2,6 +2,24 @@
 import jax.numpy as jnp
 from jax import lax
 from jax.sharding import PartitionSpec as P
+
+
+def gather_around(value, axis, dim):
+    ways, here, step = (lax.axis_size(axis), lax.axis_index(axis), value.shape[dim])
+    shape = [n * ways if d == dim else n for d, n in enumerate(value.shape)]
+    full = lax.dynamic_update_slice_in_dim(
+        jnp.zeros(shape, value.dtype), value, here * step, axis=dim
+    )
+    going_up = going_down = value
+    for far in range(1, ways // 2 + 1):
+        going_up = lax.ppermute(going_up, axis, [(d, (d + 1) % ways) for d in range(ways)])
+        full = lax.dynamic_update_slice_in_dim(full, going_up, (here - far) % ways * step, axis=dim)
+        if 2 * far < ways:
+            going_down = lax.ppermute(going_down, axis, [(d, (d - 1) % ways) for d in range(ways)])
+            full = lax.dynamic_update_slice_in_dim(
+                full, going_down, (here + far) % ways * step, axis=dim
+            )
+    return full
 
 
 def per_device(
@@ -48,7 +66,7 @@
     src_block = lax.all_gather(embeds, "col", axis=0, tiled=True)
     block_rows = owners * node_dev + local_rows
     src_embed = src_block[block_rows]
-    dst_block = lax.all_gather(embeds, "row", axis=0, tiled=True)
+    dst_block = gather_around(embeds, "row", 0)
     dst_embed = dst_block[dest_rows]
     w_src = w_first[:feat_width]
     w_dst = w_first[feat_width:]

time: 876 us -> 846 us (0.966)
  waiting for transfers between devices: 534 us -> 498 us
    all_gather x1, waiting for transfers between devices: 51.4 us -> 18.1 us  [per_device(): src_block = lax.all_gather(embeds, 'col', axis=0, tiled=True)]
    all_gather x1 -> x0, waiting for transfers between devices: 18.4 us -> none  [per_device(): dst_block = lax.all_gather(embeds, 'row', axis=0, tiled=True)]
    ppermute x0 -> x7, waiting for transfers between devices: none -> 15.9 us  [the longest x4 11.1 us: gather_around(): lax.ppermute(going_up, axis, [(d, (d + 1) % ways) for d in range(ways)])]
  transfers between devices with their start and end apart: 8 -> 14, of which waited for: 7 -> 10; matrix products, arithmetic and copies ran while one was open for 12% -> 12% of each run, Pallas kernels for 0% -> 0%
where the time goes in v1:
time: 846 us
  waiting for transfers between devices  498 us (59%)
  other arithmetic  105 us (12%)
  blocking collectives  87.6 us (10%)
  local copies, waits for them, and re-layouts  84.9 us (10%)
  matrix products  31.9 us (4%)
  starting transfers between devices  23.3 us (3%)
  between operations  15 us (2%)
    reduce_scatter x1, waiting for transfers between devices, per_device(): src_grad = lax.psum_scatter(src_acc, 'col', scatter_dimension=0, tiled=True)  222 us
    psum x1, waiting for transfers between devices, per_device(): encoder_sums = lax.psum((part_self, part_neigh, part_bsage), ('row', 'col'))  163 us
    psum x1, blocking collectives, per_device(): encoder_sums = lax.psum((part_self, part_neigh, part_bsage), ('row', 'col'))  74.7 us
    psum x1, waiting for transfers between devices, per_device(): decoder_sums = lax.psum((part_first, part_bfirst, part_second), 'row')  65.6 us
    scatter-add x1, other arithmetic, per_device(): src_acc = jnp.zeros((src_block.shape[0], feat_width), jnp.float32).at[blo...  48.3 us
    scatter-add x1, other arithmetic, per_device(): dest_acc = jnp.zeros((dst_block.shape[0], feat_width), jnp.float32).at[de...  46 us
    gather x1, local copies, waits for them, and re-layouts, per_device(): src_embed = src_block[block_rows]  33.6 us
    gather x1, local copies, waits for them, and re-layouts, per_device(): dst_embed = dst_block[dest_rows]  32.9 us
  transfers between devices with their start and end apart: 14, of which 10 were waited for; matrix products, arithmetic and copies ran while one was open for 12% of the time, Pallas kernels for 0%

profile of v1, /device:TPU:8, one launch (start us, length us, event | category | flops | bytes accessed | tf_op | source)
XLA Modules:
  0.0 845.7 jit_solution(7698776016441500474)
XLA Ops:
  7.2 0.0 copy-start
  7.2 0.7 compare_select_fusion.3
  7.9 2.5 gather_fusion
  10.5 4.4 all-to-all-start
  14.9 0.7 compare_select_fusion.2
  15.6 5.4 all-to-all-done
  21.0 0.7 copy.26
  21.8 11.7 %all-to-all-start.1 = ((bf16[1,8,32,256]{3,1,0,2:T(8,128)(2,1)}), bf16[1,8,32,256]{3,1,0,2:T(8,128)(2,1)S(1)}, u32[]{:S(2)}, u32[]{:S(2)}) async-start(bf16[1,8,32,256]{3,1,0,2:T(8,128)(2,1)} %copy.26), calls=%async_computation.1 | async-start | bytes 262144 | tf_op jit(solution)/shard_map/all_to_all | solution.py:48
  33.5 0.0 all-gather.2.cloned.1.call-start
  33.6 1.2 fusion.26
  34.8 7.8 all-to-all-done.1
  42.6 0.9 pad_maximum_fusion
  43.5 7.6 gather_fusion.1
  51.1 0.2 convert_reduce_fusion
  51.3 0.1 broadcast_in_dim.15
  51.4 0.9 constant_dynamic-update-slice_fusion.7
  52.2 0.0 all-gather.2.cloned.1.call-update
  52.3 0.2 reduce-scatter.5.cloned.1.call-start
  53.4 0.1 compare_select_fusion.1
  53.5 0.0 collective-permute-start.1
  53.6 0.5 collective-permute-start
  54.1 2.3 collective-permute-done.1
  56.4 3.0 collective-permute-start.3
  59.4 0.0 collective-permute-done
  59.4 2.5 collective-permute-done.3
  61.9 3.1 collective-permute-start.5
  65.0 0.0 collective-permute-done.2
  65.0 5.6 collective-permute-done.4
  70.6 5.5 collective-permute-done.6
  76.2 32.9 %gather_fusion.3 = bf16[8192,256]{1,0:T(8,128)(2,1)} fusion(bf16[2048,256]{1,0:T(8,128)(2,1)S(1)} %constant_dynamic-update-slice_fusion, s32[8192]{0:T(1024)S(1)} %broadcast_clamp_fusion), kind=kCustom, calls=%fused_computation.3 | custom fusion | bytes 8421376 | tf_op jit(solution)/shard_map/gather | solution.py:70
  109.1 18.1 %all-gather.2.cloned.1.call-done = bf16[8192,256]{1,0:T(8,128)(2,1)} async-done(((bf16[256,256]{1,0:T(8,128)(2,1)}), bf16[8192,256]{1,0:T(8,128)(2,1)}) %all-gather.2.cloned.1.call-update) | async-done | bytes 4194320 | tf_op jit(solution)/shard_map/all_gather | solution.py:66
  127.2 33.6 %gather_fusion.2 = bf16[8192,256]{1,0:T(8,128)(2,1)} fusion(bf16[8192,256]{1,0:T(8,128)(2,1)} %all-gather.2.cloned.1.call-done, s32[8192]{0:T(1024)S(1)} %broadcast_clamp_fusion.1), kind=kCustom, calls=%fused_computation.2 | custom fusion | bytes 8421376 | tf_op jit(solution)/shard_map/gather | solution.py:68
  160.9 3.6 fusion.16
  164.5 1.3 fusion
  165.7 2.4 fusion.6
  168.2 0.6 divide_subtract_fusion
  168.8 5.9 fusion.24
  174.7 2.0 copy-done.2
  176.6 4.5 fusion.1
  181.2 46.0 %scatter_custom_fusion.1 = f32[2048,256]{1,0:T(8,128)} fusion(s32[8192]{0:T(1024)S(1)} %bitcast.48, f32[8192,256]{1,0:T(8,128)} %fusion.1, f32[]{:T(128)} %constant.68.clone.1), kind=kCustom, calls=%fused_computation.25 | custom fusion | flops 2097152 | bytes 2097664 | tf_op jit(solution)/shard_map/scatter-add | solution.py:104
  227.2 0.0 reduce-scatter.5.cloned.1.call-update
  227.2 0.3 reduce-scatter.3.cloned.1.call-start
  227.5 6.7 fusion.2
  234.2 48.3 %scatter_custom_fusion = f32[8192,256]{1,0:T(8,128)} fusion(s32[8192]{0:T(1024)S(1)} %bitcast.46, f32[8192,256]{1,0:T(8,128)} %fusion.2, f32[]{:T(128)} %constant.68.clone.1), kind=kCustom, calls=%fused_computation.16 | custom fusion | flops 2097152 | bytes 8389120 | tf_op jit(solution)/shard_map/scatter-add | solution.py:98
  282.5 0.0 reduce-scatter.3.cloned.1.call-update
  282.5 0.0 all-reduce.7.cloned.1.call-start
  282.6 4.8 fusion.27
  287.3 0.0 reduce-scatter.5.cloned.1.call-done
  287.4 222.0 %reduce-scatter.3.cloned.1.call-done = f32[256,256]{1,0:T(8,128)} async-done(((f32[8192,256]{1,0:T(8,128)}), f32[256,256]{1,0:T(8,128)}) %reduce-scatter.3.cloned.1.call-update) | async-done | bytes 262160 | tf_op jit(solution)/shard_map/reduce_scatter | solution.py:100
  509.4 1.1 fusion.25
  510.5 0.9 fusion.18
  511.4 0.9 convolution_bitcast_fusion
  512.3 0.0 all-reduce.7.cloned.1.call-update
  512.4 0.0 all-reduce.5.cloned.1.call-start
  512.4 4.8 fusion.28
  517.2 0.8 maximum_bitcast_fusion
  518.0 0.0 all-reduce.5.cloned.1.call-update
  518.1 13.0 %all-reduce.1 = (f32[1,256]{1,0:T(1,128)}, f32[1,256]{1,0:T(1,128)}) all-reduce(f32[1,256]{1,0:T(1,128)S(1)} %bitcast.52, f32[1,256]{1,0:T(1,128)S(1)} %bitcast.53), channel_id=1, replica_groups=mesh['row'=8,'col'=32] {'row'}, use_global_device_ids=true, to_apply=%region_11.12 | all-reduce | flops 512 | bytes 4096 | tf_op jit(solution)/shard_map/psum | solution.py:88
  531.1 74.7 %psum.44 = f32[256]{0:T(256)} all-reduce(f32[256]{0:T(256)S(1)} %get-tuple-element.42), channel_id=1, replica_groups=mesh['row'=8,'col'=32] {'row','col'}, use_global_device_ids=true, to_apply=%region_8.9 | all-reduce | flops 256 | bytes 2048 | tf_op jit(solution)/shard_map/psum | solution.py:112
  605.7 162.6 %all-reduce.7.cloned.1.call-done = (f32[256,256]{0,1:T(8,128)}, f32[256,256]{1,0:T(8,128)}) async-done(((f32[256,256]{0,1:T(8,128)}, f32[256,256]{1,0:T(8,128)}), (f32[256,256]{0,1:T(8,128)}, f32[256,256]{1,0:T(8,128)})) %all-reduce.7.cloned.1.call-update) | async-done | bytes 524304 | tf_op jit(solution)/shard_map/psum | solution.py:112
  768.3 1.8 copy.28
  770.1 65.6 %all-reduce.5.cloned.1.call-done = f32[1,512,256]{2,1,0:T(8,128)} async-done(((f32[1,512,256]{2,1,0:T(8,128)}), f32[1,512,256]{2,1,0:T(8,128)}) %all-reduce.5.cloned.1.call-update) | async-done | bytes 524304 | tf_op jit(solution)/shard_map/psum | solution.py:88
  835.6 1.7 copy.41
  837.3 1.9 copy.42
  (47 shorter events, 0.3 us)
Async XLA Ops:
  7.2 44.2 %copy-start = (bf16[256,256]{1,0:T(8,128)(2,1)S(1)}, bf16[256,256]{1,0:T(8,128)(2,1)}, u32[]{:S(2)}) copy-start(bf16[256,256]{1,0:T(8,128)(2,1)} %param.18) | copy-start | bytes 393220
  10.5 40.9 %copy-start.12 = (f32[256]{0:T(256)S(1)}, f32[256]{0:T(256)}, u32[]{:S(2)}) copy-start(f32[256]{0:T(256)} %param.19) | copy-start | bytes 3076
  10.5 10.6 %all-to-all-start = ((bf16[1,8,32,256]{3,2,0,1:T(8,128)(2,1)}), bf16[1,8,32,256]{3,2,0,1:T(8,128)(2,1)S(1)}, u32[]{:S(2)}, u32[]{:S(2)}) async-start(bf16[1,8,32,256]{3,2,0,1:T(8,128)(2,1)} %bitcast.3), calls=%async_computation | async-start | bytes 262144 | tf_op jit(solution)/shard_map/all_to_all | solution.py:49
  21.8 20.8 %all-to-all-start.1 = ((bf16[1,8,32,256]{3,1,0,2:T(8,128)(2,1)}), bf16[1,8,32,256]{3,1,0,2:T(8,128)(2,1)S(1)}, u32[]{:S(2)}, u32[]{:S(2)}) async-start(bf16[1,8,32,256]{3,1,0,2:T(8,128)(2,1)} %copy.26), calls=%async_computation.1 | async-start | bytes 262144 | tf_op jit(solution)/shard_map/all_to_all | solution.py:48
  33.5 93.7 %all-gather.2.cloned.1.call-start = ((), (), s32[]{:S(2)}) async-start(), calls=%async_computation.4 | async-start | bytes 4325376 | tf_op jit(solution)/shard_map/all_gather | solution.py:66
  33.5 19.1 %copy-start.13 = (bf16[256]{0:T(256)(128)(2,1)S(1)}, bf16[256]{0:T(256)(128)(2,1)}, u32[]{:S(2)}) copy-start(bf16[256]{0:T(256)(128)(2,1)} %param.22) | copy-start | bytes 1540
  33.6 19.7 %copy-start.9 = (s32[1,1,8192]{2,1,0:T(1,128)S(1)}, s32[1,1,8192]{2,1,0:T(1,128)}, u32[]{:S(2)}) copy-start(s32[1,1,8192]{2,1,0:T(1,128)} %param.27) | copy-start | bytes 98308
  34.7 18.6 %copy-start.7 = (s32[1,1,8192]{2,1,0:T(1,128)S(1)}, s32[1,1,8192]{2,1,0:T(1,128)}, u32[]{:S(2)}) copy-start(s32[1,1,8192]{2,1,0:T(1,128)} %param.25) | copy-start | bytes 98308
  34.7 18.6 %copy-start.8 = (s32[1,1,8192,1]{2,3,1,0:T(1,128)S(1)}, s32[1,1,8192,1]{2,3,1,0:T(1,128)}, u32[]{:S(2)}) copy-start(s32[1,1,8192,1]{2,3,1,0:T(1,128)} %param.24) | copy-start | bytes 98308
  34.8 18.7 %copy-start.10 = (s32[1,1,8192]{2,1,0:T(1,128)S(1)}, s32[1,1,8192]{2,1,0:T(1,128)}, u32[]{:S(2)}) copy-start(s32[1,1,8192]{2,1,0:T(1,128)} %param.26) | copy-start | bytes 98308
  52.3 235.1 %reduce-scatter.5.cloned.1.call-start = ((), (), s32[]{:S(2)}) async-start(), calls=%async_computation.6 | async-start | bytes 2359296 | tf_op jit(solution)/shard_map/reduce_scatter | solution.py:106
  53.5 2.9 collective-permute-start.1
  53.6 5.8 collective-permute-start
  56.4 5.5 collective-permute-start.3
  59.4 5.6 collective-permute-start.2
  61.9 8.7 %collective-permute-start.5 = (bf16[256,256]{1,0:T(8,128)(2,1)S(1)}, bf16[256,256]{1,0:T(8,128)(2,1)S(1)}, u32[]{:S(2)}, u32[]{:S(2)}) collective-permute-start(bf16[256,256]{1,0:T(8,128)(2,1)S(1)} %collective-permute-done.3), channel_id=1, source_target_pairs={{0,224},{32,0},{64,32},{96,64},{128,96},{160,128},{192,160},{224,1... | collective-permute-start | bytes 393224 | tf_op jit(solution)/shard_map/ppermute | solution.py:18
  65.0 5.6 collective-permute-start.4
  70.6 5.6 collective-permute-start.6
  109.1 51.8 %copy-start.6 = (bf16[512,256]{1,0:T(8,128)(2,1)S(1)}, bf16[512,256]{1,0:T(8,128)(2,1)}, u32[]{:S(2)}) copy-start(bf16[512,256]{1,0:T(8,128)(2,1)} %param.20) | copy-start | bytes 786436
  160.9 3.6 copy-start.3
  160.9 3.6 copy-start.11
  174.7 2.0 copy-start.2
  227.2 282.2 %reduce-scatter.3.cloned.1.call-start = ((), (), s32[]{:S(2)}) async-start(), calls=%async_computation.5 | async-start | bytes 8650752 | tf_op jit(solution)/shard_map/reduce_scatter | solution.py:100
  282.5 228.9 %copy-start.4 = (bf16[256,256]{1,0:T(8,128)(2,1)S(1)}, bf16[256,256]{1,0:T(8,128)(2,1)}, u32[]{:S(2)}) copy-start(bf16[256,256]{1,0:T(8,128)(2,1)} %param.14) | copy-start | bytes 393220
  282.5 485.8 %all-reduce.7.cloned.1.call-start = ((), (), s32[]{:S(2)}) async-start(), calls=%async_computation.8 | async-start | bytes 1048576 | tf_op jit(solution)/shard_map/psum | solution.py:112
  510.5 6.7 copy-start.5
  512.4 326.8 %copy-start.1 = (bf16[256,256]{1,0:T(8,128)(2,1)S(1)}, bf16[256,256]{1,0:T(8,128)(2,1)}, u32[]{:S(2)}) copy-start(bf16[256,256]{1,0:T(8,128)(2,1)} %param.18) | copy-start | bytes 393220
  512.4 323.3 %all-reduce.5.cloned.1.call-start = ((), (), s32[]{:S(2)}) async-start(), calls=%async_computation.7 | async-start | bytes 1048576 | tf_op jit(solution)/shard_map/psum | solution.py:88
Sparse Core Ops, SparseCore 0:
  52.4 74.7 all-gather.1
  227.3 34.6 reduce-scatter.4
  282.6 226.7 reduce-scatter.2
  516.4 251.8 all-reduce.6
  771.2 64.4 all-reduce.4
